TPU v7x, 32 devices: a whole 2x2x4 slice. The times are simulated.
32 devices in a mesh: rows: 16 (over z, x, core), batch: 2 (over y).
Axes of the slice: x: 2, y: 2, z: 4, core: 2. Of those that a mesh axis runs over, the one named last changes fastest.
Arguments:
- features: bfloat16 [3, 8, 32, 64, 384], P(None, 'batch', 'rows'), may hold values from -6 to 6
- drop_mask: int32 [3, 8], P(None, 'batch'), may hold values 0 or 1
- labels: int32 [3, 8], P(None, 'batch'), may hold values from 0 to 999
- params: float32 [3153920], P('rows'), may hold values from -4 to 4, as said below
- moment1: float32 [3153920], P('rows'), may hold values from -1 to 1, as said below
- moment2: float32 [3153920], P('rows'), may hold values from 0 to 1, as said below
Outputs:
- new_params: float32 [3153920], P('rows')
- new_moment1: float32 [3153920], P('rows')
- new_moment2: float32 [3153920], P('rows')
- loss_sum: float32 [], replicated
- grad_norm: float32 [], replicated
- feature_grad: float32 [3, 8, 32, 64, 384], P(None, 'batch', 'rows')
Inputs may be any that keep to these rules, and one draw needn't show every extreme that they name: `params`: master parameters laid out as the steps say; gains near one, weights scaled by fan-in. `moment1`: first moments of both signs. `moment2`: positive second moments.
All inputs are finite; a program needn't handle non-finite values. No bound on the sum of `drop_mask` on one device may be relied on, other than what follows from the above.
Results may differ from a plain program's by a relative error of at most 0.0073.
Values may be sent and summed in bfloat16 or wider, within the bound.
A program may use at most 256 MiB of HBM per device.

v0:
```python
import functools

import jax
import jax.numpy as jnp
from jax import lax
from jax.experimental import pallas as pl
from jax.experimental.pallas import tpu as pltpu
from jax.sharding import PartitionSpec as P

C = 384
HID = 1536
DOUT = 768
CLS = 1000
MICRO = 3
STEP = 10
P_SIZE = 3153920
KEEP = 0.8
CLIP = 0.01
RATE = 0.05
BETA_ONE = 0.9
BETA_TWO = 0.999
DECAY = 0.05
EPS_ADAM = 1e-08
EPS_NORM = 1e-06

MESH = pl.DeviceIdType.MESH
F32 = jnp.float32
BF16 = jnp.bfloat16
MB = 1 << 20

LANES = 128
J = C // LANES
GROUP = 4
OWN = 8
COLS = 64
PADC = COLS + 6
SUB = 16
POS = COLS * OWN
NPOS = MICRO * POS
FLAT = P_SIZE // LANES
ROW_K = 0
ROW_UP = 49 * J
ROW_CUP = ROW_UP + C * HID // LANES
ROW_DOWN = ROW_CUP + HID // LANES
ROW_VEC = ROW_DOWN + C * HID // LANES
ROW_DS = ROW_VEC + 7 * J
ROW_OUT = ROW_DS + 4 * C * DOUT // LANES
ROW_HEAD = ROW_OUT + 3 * DOUT // LANES
ROW_BH = ROW_HEAD + DOUT * CLS // LANES
TABLES = (
    (ROW_K, 49 * J, 0),
    (ROW_CUP, HID // LANES, 152),
    (ROW_VEC, 7 * J, 168),
    (ROW_OUT, 3 * DOUT // LANES, 192),
    (ROW_BH, FLAT - ROW_BH, 216),
)
TAB_ROWS = 232
TAB_SPAN = (152, 16, 24, 24, 16)
T_CUP, T_VEC, T_OUT, T_BH = 152, 168, 192, 216
SG_ROWS = 320
SG_VEC, SG_CUP = 160, 240
CLSP = 1024


class Env:
    pass


def xrow(j, m):
    return (j * MICRO + m) * PADC * SUB


def rows_of(refs, row, count):
    return refs[row : row + count, :]


def lane_row(ref, row, count):
    return jnp.concatenate([ref[row + k : row + k + 1, :] for k in range(count)], axis=1)


def ln_parts(blocks, width):
    total = blocks[0]
    for block in blocks[1:]:
        total = total + block
    mean = jnp.sum(total, -1, keepdims=True) * (1.0 / width)
    centred = [block - mean for block in blocks]
    square = centred[0] * centred[0]
    for block in centred[1:]:
        square = square + block * block
    spread = jnp.sum(square, -1, keepdims=True) * (1.0 / width)
    scale = lax.rsqrt(spread + EPS_NORM)
    return [block * scale for block in centred], scale


def here(e):
    e.r = lax.axis_index("rows")
    e.b = lax.axis_index("batch")
    e.g = e.r // GROUP
    e.i = e.r % GROUP
    e.h = e.b % 2


def dev(e, r=None, b=None):
    return {"rows": e.r if r is None else r, "batch": e.b if b is None else b}


def remote(e, src, dst, send, recv, r=None, b=None):
    return pltpu.make_async_remote_copy(
        src, dst, send, recv, device_id=(e.r if r is None else r, e.b if b is None else b), device_id_type=MESH
    )


def ph_barrier_signal(e, B):
    barrier = pltpu.get_barrier_semaphore()
    for d in range(1, e.n):
        pl.semaphore_signal(barrier, inc=1, device_id=(lax.rem(e.r + d, e.n), e.b), device_id_type=MESH)
    for d in range(1, e.nb):
        pl.semaphore_signal(barrier, inc=1, device_id=(e.r, lax.rem(e.b + d, e.nb)), device_id_type=MESH)


def ph_barrier_wait(e, B):
    pl.semaphore_wait(pltpu.get_barrier_semaphore(), e.n - 1 + e.nb - 1)


def feat_copy(e, B, m, d):
    j = lax.rem(e.i + d, GROUP)
    return remote(
        e,
        B.features.at[m, j],
        B.xg.at[m, pl.ds(3 + 2 * e.i, 2)],
        B.s_feat.at[m, d],
        B.r_feat.at[m, d],
        r=e.g * GROUP + j,
    )


def feat_own(e, B):
    return pltpu.make_async_copy(B.features.at[:, e.i], B.xg.at[:, pl.ds(3 + 2 * e.i, 2)], B.s_own.at[0])


def feat_start(e, B, m):
    if m == 0:
        feat_own(e, B).start()
    for d in (2, 3, 1):
        feat_copy(e, B, m, d).start()


def ph_feat_zero(e, B):
    zero = jnp.zeros((MICRO, 3, COLS, C), BF16)

    @pl.when(e.g == 0)
    def _():
        B.xg[:, 0:3] = zero

    @pl.when(e.g == e.G - 1)
    def _():
        B.xg[:, 11:14] = zero


def halo_copy(e, B, m, up):
    if up:
        return remote(e, B.xg.at[m, 8:11], B.xg.at[m, 0:3], B.s_halo.at[1, m], B.r_halo.at[1, m], r=e.r + GROUP)
    return remote(e, B.xg.at[m, 3:6], B.xg.at[m, 11:14], B.s_halo.at[0, m], B.r_halo.at[0, m], r=e.r - GROUP)


def halo_start(e, B, m):
    if m == 0:
        feat_own(e, B).wait()
    for d in range(1, GROUP):
        feat_copy(e, B, m, d).wait_recv()

    @pl.when(e.g > 0)
    def _():
        halo_copy(e, B, m, False).start()

    @pl.when(e.g < e.G - 1)
    def _():
        halo_copy(e, B, m, True).start()


def halo_wait(e, B, m):
    @pl.when(e.g < e.G - 1)
    def _():
        halo_copy(e, B, m, False).wait_recv()

    @pl.when(e.g > 0)
    def _():
        halo_copy(e, B, m, True).wait_recv()


def ph_feat_done(e, B):
    for m in range(MICRO):
        for d in range(1, GROUP):
            feat_copy(e, B, m, d).wait_send()

        @pl.when(e.g > 0)
        def _(m=m):
            halo_copy(e, B, m, False).wait_send()

        @pl.when(e.g < e.G - 1)
        def _(m=m):
            halo_copy(e, B, m, True).wait_send()


def ph_cast(e, B):
    for h in range(2):
        count = e.half if h == 0 else e.slab - e.half
        whole = count // 16 * 16
        B.gw[e.r, h, 0:whole, :] = B.params[h * e.half : h * e.half + whole, :].astype(BF16)
        rest = count - whole
        if whole < e.half:
            parts = [jnp.zeros((e.half - whole - rest, LANES), F32)]
            if rest:
                parts = [B.params[e.slab - rest : e.slab, :]] + parts
            B.gw[e.r, h, whole : e.half, :] = jnp.concatenate(parts, axis=0).astype(BF16)
    for k, (first, count, place) in enumerate(TABLES):
        off = first % e.slab

        @pl.when(e.r == first // e.slab)
        def _(off=off, count=count, place=place):
            B.tab[place : place + count, :] = B.params[off : off + count, :]


def table_line(e, B, k, d):
    first, count, place = TABLES[k]
    owner = first // e.slab
    part = pl.ds(place, TAB_SPAN[k])
    return remote(e, B.tab.at[part], B.tab.at[part], B.s_tab.at[k, d], B.r_tab.at[k], r=lax.rem(owner + GROUP * d, e.n))


def table_group(e, B, k, d):
    first, count, place = TABLES[k]
    part = pl.ds(place, TAB_SPAN[k])
    to = e.g * GROUP + lax.rem(e.i + d, GROUP)
    return remote(e, B.tab.at[part], B.tab.at[part], B.s_tabg.at[k, d], B.r_tab.at[k], r=to)


def ph_tables_start(e, B):
    for k, (first, count, place) in enumerate(TABLES):
        owner = first // e.slab

        @pl.when(e.r == owner)
        def _(k=k):
            for d in range(1, e.G):
                table_line(e, B, k, d).start()
            for d in range(1, GROUP):
                table_group(e, B, k, d).start()


def tables_forward(e, B, some):
    for k in some:
        owner = TABLES[k][0] // e.slab

        @pl.when(jnp.logical_and(e.i == owner % GROUP, e.r != owner))
        def _(k=k):
            table_line(e, B, k, 1).wait_recv()
            for d in range(1, GROUP):
                table_group(e, B, k, d).start()


def tables_wait(e, B, some):
    for k in some:
        owner = TABLES[k][0] // e.slab

        @pl.when(e.i != owner % GROUP)
        def _(k=k):
            table_group(e, B, k, 1).wait_recv()


def ph_tables_done(e, B):
    for k, (first, count, place) in enumerate(TABLES):
        owner = first // e.slab

        @pl.when(e.r == owner)
        def _(k=k):
            for d in range(1, e.G):
                table_line(e, B, k, d).wait_send()

        @pl.when(e.i == owner % GROUP)
        def _(k=k):
            for d in range(1, GROUP):
                table_group(e, B, k, d).wait_send()


CHUNKS = 4


def chunk_of(e, c):
    if c is None:
        return pl.ds(0, e.half)
    tiles = e.half // 16
    cuts = [(tiles * k + CHUNKS - 1) // CHUNKS * 16 for k in range(CHUNKS + 1)]
    return pl.ds(cuts[c], cuts[c + 1] - cuts[c])


def half_ref(e, B, slot, h, c):
    return B.gw.at[slot, h, chunk_of(e, c)]


def line_copy(e, B, level, up, c):
    ref = half_ref(e, B, level * GROUP + e.i, e.h, c)
    k = 0 if up else 1
    return remote(e, ref, ref, B.s_line.at[k, level], B.r_line.at[level, c or 0], r=e.r + GROUP if up else e.r - GROUP)


def pair_copy(e, B, level, c):
    ref = half_ref(e, B, level * GROUP + e.i, e.h, c)
    to = e.g * GROUP + lax.rem(e.i + 2, GROUP)
    return remote(e, ref, ref, B.s_pair.at[level], B.r_pair.at[level, c or 0], r=to)


def row_copy(e, B, level, other, c):
    i = lax.rem(e.i + 2, GROUP) if other else e.i
    ref = half_ref(e, B, level * GROUP + i, e.h, c)
    k = int(other)
    return remote(e, ref, ref, B.s_row.at[k, level], B.r_row.at[k, level, c or 0], b=e.b + 1 - 2 * e.h)


def core_copy(e, B, level, other, mine, c):
    i = lax.rem(e.i + 2, GROUP) if other else e.i
    ref = half_ref(e, B, level * GROUP + i, e.h if mine else 1 - e.h, c)
    k = 2 * int(other) + int(mine)
    sib = e.g * GROUP + e.i + 1 - 2 * (e.i % 2)
    return remote(e, ref, ref, B.s_core.at[k, level], B.r_core.at[k, level, c or 0], r=sib)


def line_out(e, B, level, c):
    @pl.when(jnp.logical_and(e.g >= level, e.g + 1 < e.G))
    def _():
        line_copy(e, B, level, True, c).start()

    @pl.when(jnp.logical_and(e.g <= level, e.g >= 1))
    def _():
        line_copy(e, B, level, False, c).start()


def at_hop(e, level, hop, body):
    if hop == 0:
        cond = e.g == level
    else:
        cond = jnp.logical_or(e.g == level + hop, e.g == level - hop)
    pl.when(cond)(body)


def line_send(e, B, levels, chunks):
    for level in levels:

        def body(level=level):
            for c in chunks:
                line_out(e, B, level, c)

        at_hop(e, level, 0, body)


def line_step(e, B, levels, hop, chunks):
    for level in levels:

        def body(level=level):
            for c in chunks:
                line_copy(e, B, level, True, c).wait_recv()
                line_out(e, B, level, c)
                row_copy(e, B, level, False, c).start()
                core_copy(e, B, level, False, True, c).start()

        at_hop(e, level, hop, body)


def pair_step(e, B, levels, hop, chunks):
    for level in levels:

        def body(level=level):
            for c in chunks:
                pair_copy(e, B, level, c).start()
                if hop == 0:
                    core_copy(e, B, level, False, True, c).start()
                    core_copy(e, B, level, False, False, c).start()

        at_hop(e, level, hop, body)


def row_step(e, B, levels, hop, chunks):
    for level in levels:

        def body(level=level):
            for c in chunks:
                pair_copy(e, B, level, c).wait_recv()
                row_copy(e, B, level, True, c).start()
                core_copy(e, B, level, True, True, c).start()

        at_hop(e, level, hop, body)


def core_step(e, B, levels, hop, chunks):
    for level in levels:

        def body(level=level):
            for c in chunks:
                if hop:
                    row_copy(e, B, level, False, c).wait_recv()
                    core_copy(e, B, level, False, False, c).start()
                row_copy(e, B, level, True, c).wait_recv()
                core_copy(e, B, level, True, False, c).start()

        at_hop(e, level, hop, body)


def gather_ready(e, B, levels):
    for level in levels:
        for other in (False, True):
            for mine in (False, True):
                for c in range(CHUNKS):
                    core_copy(e, B, level, other, mine, c).wait_recv()


def ph_gather_done(e, B):
    G = e.G
    for level in range(G):
        pair_copy(e, B, level, None).wait_send()
        row_copy(e, B, level, True, None).wait_send()

        @pl.when(e.g != level)
        def _(level=level):
            row_copy(e, B, level, False, None).wait_send()

        for other in (False, True):
            for mine in (False, True):
                core_copy(e, B, level, other, mine, None).wait_send()

        @pl.when(jnp.logical_and(e.g >= level, e.g + 1 < G))
        def _(level=level):
            line_copy(e, B, level, True, None).wait_send()

        @pl.when(jnp.logical_and(e.g <= level, e.g >= 1))
        def _(level=level):
            line_copy(e, B, level, False, None).wait_send()


def flatten(e, B, first, last):
    s0 = first // e.slab

    def slab(k, _):
        for h in range(2):
            count = (e.half if h == 0 else e.slab - e.half + 15) // 16 * 16
            base = e.slab * k + h * e.half
            B.big[pl.ds(base, count), :] = B.gw[s0 + k, h, 0:count, :].astype(F32)
        return 0

    lax.fori_loop(0, (last - 1) // e.slab - s0 + 1, slab, 0)
    return e.slab * s0


def ph_weights_up(e, B):
    base = flatten(e, B, ROW_UP, ROW_CUP)
    for j in range(HID // LANES):
        B.wup[:, LANES * j : LANES * (j + 1)] = B.big[pl.ds(ROW_UP - base + j, C, stride=HID // LANES), :].astype(BF16)


def ph_weights_down(e, B):
    base = flatten(e, B, ROW_DOWN, ROW_VEC)
    for j in range(J):
        B.wdn[:, LANES * j : LANES * (j + 1)] = B.big[pl.ds(ROW_DOWN - base + j, HID, stride=J), :].astype(BF16)


def ph_weights_head(e, B):
    base = flatten(e, B, ROW_DS, ROW_OUT)
    per = DOUT // LANES
    for j in range(per):
        B.wds[:, LANES * j : LANES * (j + 1)] = B.big[pl.ds(ROW_DS - base + j, 4 * C, stride=per), :].astype(BF16)
    base = flatten(e, B, ROW_HEAD, ROW_BH)
    lane = lax.broadcasted_iota(jnp.int32, (DOUT // 16, LANES), 1)
    for kk in range(16):
        first, off = divmod(CLS * kk, LANES)
        parts = [B.big[pl.ds(ROW_HEAD - base + first + t, DOUT // 16, stride=125), :] for t in range(9 if off else 8)]
        if off:
            parts = [pltpu.roll(part, LANES - off, 1) for part in parts]
        for t in range(8):
            tile = parts[t]
            if off:
                tile = jnp.where(lane < LANES - off, parts[t], parts[t + 1])
            if t == 7:
                tile = jnp.where(lane < CLS - 7 * LANES, tile, 0.0)
            B.dx[pl.ds(DOUT * t + kk, DOUT // 16, stride=16), :] = tile
    for t in range(8):
        B.wh[:, LANES * t : LANES * (t + 1)] = B.dx[DOUT * t : DOUT * (t + 1), :].astype(BF16)


def hooks(it, steps, also=None):
    if not steps:
        return
    bits = sum(1 << k for k in steps)
    due = lax.rem(lax.shift_right_logical(jnp.int32(bits), it), 2) == 1
    if also is not None:
        due = jnp.logical_and(due, also)

    @pl.when(due)
    def _():
        for k, some in steps.items():

            @pl.when(it == k)
            def _(some=some):
                for step in some:
                    step()


def transpose(e, B, m):
    pad = jnp.zeros((3 * SUB, LANES), F32)
    for j in range(J):
        B.big[pl.ds(xrow(j, m), 3 * SUB), :] = pad
        B.big[pl.ds(xrow(j, m) + (COLS + 3) * SUB, 3 * SUB), :] = pad
        for row in range(14):
            v = B.xg[m, row, :, LANES * j : LANES * (j + 1)].astype(F32)
            B.big[pl.ds(xrow(j, m) + 3 * SUB + row, COLS, stride=SUB), :] = v
            if 3 <= row < 11:
                B.xc[pl.ds(j * NPOS + m * POS + row - 3, COLS, stride=OWN), :] = v


def ph_taps(e, B):
    def body(t, _):
        B.kb[t] = jnp.broadcast_to(B.tab[pl.ds(t, 1), :], (8, LANES))
        return 0

    lax.fori_loop(0, 49 * J, body, 0)


def vec_row(B, v, j):
    row = T_VEC + v * J + j
    return B.tab[row : row + 1, :]


def conv_tile(B, m, j, c0, tile, acc, flip):
    for a in range(7):
        taps = [B.kb[((6 - a) * 7 + 6 - b if flip else a * 7 + b) * J + j] for b in range(7)]
        for c in range(tile + 6):
            d = B.big[pl.ds(xrow(j, m) + (c0 + c) * SUB + a, OWN), :]
            for b in range(7):
                if 0 <= c - b < tile:
                    acc[c - b] = acc[c - b] + d * taps[b]
    return acc


TILE = 32


def ph_conv_fwd(e, B, steps):
    halves = COLS // TILE

    def body(it, _):
        m = it // halves
        c0 = it % halves * TILE
        for j in range(J):
            hooks(it, {k // J: v for k, v in steps.items() if k % J == j})
            bias = jnp.broadcast_to(vec_row(B, 0, j), (OWN, LANES))
            acc = conv_tile(B, m, j, c0, TILE, [bias] * TILE, False)
            at = j * NPOS + m * POS + c0 * OWN
            for c in range(TILE):
                B.dx[pl.ds(pl.multiple_of(at + OWN * c, OWN), OWN), :] = acc[c]
        return 0

    lax.fori_loop(0, MICRO * halves, body, 0)


def ph_norm_one(e, B):
    size = 256

    def body(it, _):
        at = pl.multiple_of(it * size, size)
        hat, scale = ln_parts([B.dx[pl.ds(j * NPOS + at, size), :] for j in range(J)], C)
        B.rs1[pl.ds(at, size), :] = jnp.broadcast_to(scale, (size, LANES))
        for j in range(J):
            B.v1[pl.ds(at, size), LANES * j : LANES * (j + 1)] = hat[j]
            B.n[pl.ds(at, size), LANES * j : LANES * (j + 1)] = (
                hat[j] * vec_row(B, 1, j) + vec_row(B, 2, j)
            ).astype(BF16)
        return 0

    lax.fori_loop(0, NPOS // size, body, 0)


def ph_mlp_up(e, B, steps):
    chunk = 256
    width = 256
    c0 = 0.7978845608028654
    c1 = 0.044715 * c0

    def body(it, _):
        hooks(it, steps)
        at = pl.multiple_of(it * chunk, chunk)
        rows = B.n[pl.ds(at, chunk), :]
        for k in range(HID // width):
            lanes = slice(width * k, width * (k + 1))
            bias = lane_row(B.tab, T_CUP + k * width // LANES, width // LANES)
            h = jnp.dot(rows, B.wup[:, lanes], preferred_element_type=F32) + bias
            sq = h * h
            half = 0.5 * jnp.tanh(h * (c0 + c1 * sq)) + 0.5
            u = h * half
            B.u[pl.ds(at, chunk), lanes] = u.astype(BF16)
            slope = half + u * (1.0 - half) * (2.0 * c0 + 6.0 * c1 * sq)
            B.gp[pl.ds(at, chunk), lanes] = slope.astype(BF16)
        return 0

    lax.fori_loop(0, NPOS // chunk, body, 0)


def ph_mlp_down(e, B, steps):
    chunk = 256
    B.ps[...] = jnp.zeros_like(B.ps)

    def body(it, _):
        hooks(it, steps)
        at = pl.multiple_of(it * chunk, chunk)
        m = it // (POS // chunk)
        keep = B.mask[m, e.i].astype(F32) * (1.0 / KEEP)
        z = jnp.dot(B.u[pl.ds(at, chunk), :], B.wdn[...], preferred_element_type=F32)
        resid = []
        for j in range(J):
            zj = z[:, LANES * j : LANES * (j + 1)] + vec_row(B, 3, j)
            B.z[pl.ds(j * NPOS + at, chunk), :] = zj
            resid.append(B.xc[pl.ds(j * NPOS + at, chunk), :] + (vec_row(B, 4, j) * keep) * zj)
        hat, scale = ln_parts(resid, C)
        B.rs2[pl.ds(at, chunk), :] = jnp.broadcast_to(scale, (chunk, LANES))
        for j in range(J):
            B.v2[pl.ds(at, chunk), LANES * j : LANES * (j + 1)] = hat[j]
            low = (hat[j] * vec_row(B, 5, j) + vec_row(B, 6, j)).astype(BF16).astype(F32)
            low = jnp.sum(low.reshape(chunk // 16, 2, OWN, LANES), 0)
            B.ps[m, :, :, LANES * j : LANES * (j + 1)] += low
        return 0

    lax.fori_loop(0, NPOS // chunk, body, 0)


def ph_patch_local(e, B):
    even = lax.broadcasted_iota(jnp.int32, (OWN, C), 0) % 2 == 0
    pick = lax.broadcasted_iota(jnp.int32, (8, C), 0)
    for parity in range(2):
        tile = jnp.zeros((8, C), F32)
        for side in range(2):
            for m in range(MICRO):
                v = B.ps[m, side]
                part = jnp.sum(jnp.where(even if parity == 0 else jnp.logical_not(even), v, 0.0), 0, keepdims=True)
                tile = jnp.where(pick == m + 4 * side, part, tile)
        B.sl[8 * parity : 8 * parity + 8, :] = tile


def place_rows(sums, q):
    tile = sums[8 * (q // 2) : 8 * (q // 2) + 8, :]
    return pltpu.roll(tile, 4, 0) if q % 2 else tile


def patch_copy(e, B, d):
    to = lax.rem(e.g + d, e.G)
    return remote(e, B.sl, B.sr.at[d], B.s_patch.at[d], B.r_patch.at[d], r=to * GROUP + e.i)


def patch_start(e, B):
    for d in range(1, e.G):
        patch_copy(e, B, d).start()
    B.sr[0] = B.sl[...]


def patch_wait(e, B):
    for d in range(1, e.G):
        patch_copy(e, B, d).wait_recv()
    for d in range(1, e.G):
        patch_copy(e, B, d).wait_send()


def split3(v):
    hi = v.astype(BF16).astype(F32)
    mid = (v - hi).astype(BF16).astype(F32)
    return hi, mid, v - hi - mid


def ph_head(e, B):
    total = None
    for level in range(e.G):
        part = B.sr[lax.rem(e.g - level + e.G, e.G)]
        total = part if total is None else total + part
    per = DOUT // LANES
    gain = lane_row(B.tab, T_OUT + per, per)
    shift = lane_row(B.tab, T_OUT + 2 * per, per)
    mean = total * (1.0 / e.positions)
    pooled = lane_row(B.tab, T_OUT, per)
    for q in range(4):
        parts = jnp.concatenate(split3(place_rows(mean, q)), axis=0).astype(BF16)
        prod = jnp.dot(parts, B.wds[C * q : C * (q + 1), :], preferred_element_type=F32)
        pooled = pooled + (prod[0:8] + (prod[8:16] + prod[16:24]))
    rows = lax.broadcasted_iota(jnp.int32, (8, 1), 0)
    live = rows < MICRO
    (hat,), scale = ln_parts([pooled], DOUT)
    query = (hat * gain + shift).astype(BF16)
    lane = lax.broadcasted_iota(jnp.int32, (8, CLSP), 1)
    logits = jnp.dot(query, B.wh[...], preferred_element_type=F32) + lane_row(B.tab, T_BH, CLSP // LANES)
    logits = jnp.where(lane < CLS, logits, -1e30)
    top = jnp.max(logits, 1, keepdims=True)
    powers = jnp.exp(logits - top)
    expsum = jnp.sum(powers, 1, keepdims=True)
    label = jnp.zeros((8, 1), jnp.int32)
    for m in range(MICRO):
        label = jnp.where(rows == m, B.labels[m, e.i], label)
    onehot = (lane == label).astype(F32)
    own = jnp.sum(jnp.where(lane == label, logits, 0.0), 1, keepdims=True)
    loss = jnp.sum(jnp.where(live, top + jnp.log(expsum) - own, 0.0), 0, keepdims=True)
    grad = jnp.where(live, (powers / expsum - onehot) * e.inv_count, 0.0).astype(BF16)
    grad_query = lax.dot_general(grad, B.wh[...], (((1,), (1,)), ((), ())), preferred_element_type=F32)
    dn = grad_query * gain
    m1 = jnp.sum(dn, 1, keepdims=True) * (1.0 / DOUT)
    m2 = jnp.sum(dn * hat, 1, keepdims=True) * (1.0 / DOUT)
    grad_pool = scale * (dn - m1 - hat * m2)
    down = jnp.where(live, grad_pool * (1.0 / e.positions), 0.0).astype(BF16)
    for q in range(4):
        B.dn2[8 * q : 8 * q + 8, :] = lax.dot_general(
            down, B.wds[C * q : C * (q + 1), :], (((1,), (1,)), ((), ())), preferred_element_type=F32
        )
    low = grad.astype(F32)
    d32 = down.astype(F32)
    q32 = jnp.where(live, query.astype(F32), 0.0)
    zero3 = jnp.zeros((3, C), F32)
    g3 = jnp.sum(jnp.where(live, grad_query * hat, 0.0), 0, keepdims=True)
    s3 = jnp.sum(jnp.where(live, grad_query, 0.0), 0, keepdims=True)
    vec = jnp.concatenate([g3, s3], axis=1)
    vec_parts = split3(vec)
    loss_parts = split3(loss)
    for q in range(4):
        at = slice(C * q, C * (q + 1))
        s_hi, s_mid, _ = split3(place_rows(total, q))
        B.pb[0:8, at] = jnp.zeros((8, C), F32)
        B.pb[8:16, at] = jnp.zeros((8, C), F32)
        B.pb[0:3, at] = s_hi[0:3]
        B.pb[3:6, at] = s_mid[0:3]
    B.pb[6:9, 0:DOUT] = d32[0:3]
    B.pb[6:9, DOUT : 2 * DOUT] = q32[0:3]
    B.pb[9:12, 0:CLSP] = low[0:3]
    for k in range(3):
        B.pb[12 + k : 13 + k, :] = vec_parts[k]
        B.pb[15:16, LANES * k : LANES * (k + 1)] = jnp.broadcast_to(loss_parts[k], (1, LANES))
    B.pall[e.i * e.nb + e.b] = B.pb[...].astype(BF16)
    even = lax.broadcasted_iota(jnp.int32, (OWN, C), 0) % 2 == 0
    for m in range(MICRO):
        for side in range(2):
            first = B.dn2[8 * side + m : 8 * side + m + 1, :]
            second = B.dn2[8 * (2 + side) + m : 8 * (2 + side) + m + 1, :]
            B.dnt[m, side] = jnp.where(even, first, second)


def batch_copy(e, B, d):
    slot = e.i * e.nb + e.b
    return remote(e, B.pall.at[slot], B.pall.at[slot], B.s_pb.at[d], B.r_pb.at[d], b=lax.rem(e.b + d, e.nb))


def group_copy(e, B, d):
    at = pl.ds(e.i * e.nb, e.nb)
    to = e.g * GROUP + lax.rem(e.i + d, GROUP)
    return remote(e, B.pall.at[at], B.pall.at[at], B.s_pg.at[d], B.r_pg.at[d], r=to)


def ph_payload_batch(e, B):
    for d in range(1, e.nb):
        batch_copy(e, B, d).start()


def ph_payload_group(e, B):
    for d in range(1, e.nb):
        batch_copy(e, B, d).wait_recv()
    for d in range(1, GROUP):
        group_copy(e, B, d).start()


def ph_payload_wait(e, B):
    for d in range(1, GROUP):
        group_copy(e, B, d).wait_recv()
    for d in range(1, e.nb):
        batch_copy(e, B, d).wait_send()
    for d in range(1, GROUP):
        group_copy(e, B, d).wait_send()


def lane_sum(blocks):
    total = blocks[0]
    for block in blocks[1:]:
        total = total + block
    return jnp.sum(total, -1, keepdims=True) * (1.0 / C)


def fold8(v):
    return jnp.sum(v.reshape(v.shape[0] // 8, 8, v.shape[1]), 0)


def ph_bwd_one(e, B):
    chunk = 256
    half = chunk // 16
    B.acc[...] = jnp.zeros_like(B.acc)
    B.acup[...] = jnp.zeros_like(B.acup)
    B.ps[...] = jnp.zeros_like(B.ps)

    def body(it, _):
        at = pl.multiple_of(it * chunk, chunk)
        m = it // (POS // chunk)
        keep = B.mask[m, e.i].astype(F32) * (1.0 / KEEP)
        span = pl.ds(at, chunk)
        lanes = [slice(LANES * j, LANES * (j + 1)) for j in range(J)]
        dg = [B.dnt[m, :, :, lanes[j]] * vec_row(B, 5, j) for j in range(J)]
        m1 = lane_sum(dg)
        hat = [B.v2[span, lanes[j]].reshape(half, 2, OWN, LANES) for j in range(J)]
        m2 = lane_sum([dg[j] * hat[j] for j in range(J)])
        scale = B.rs2[span, :].reshape(half, 2, OWN, LANES)
        for j in range(J):
            zspan = pl.ds(j * NPOS + at, chunk)
            dr = (scale * (dg[j] - m1 - hat[j] * m2)).reshape(chunk, LANES)
            B.ps[m, :, :, lanes[j]] += jnp.sum(hat[j], 0)
            dz = (dr * (vec_row(B, 4, j) * keep)).astype(BF16)
            B.dz[span, lanes[j]] = dz
            B.acc[3, :, lanes[j]] += fold8(dz.astype(F32))
            B.acc[4, :, lanes[j]] += fold8(dr * B.z[zspan, :]) * keep
            B.z[zspan, :] = dr
        return 0

    lax.fori_loop(0, NPOS // chunk, body, 0)
    for m in range(MICRO):
        B.acc[5] += B.dnt[m, 0] * B.ps[m, 0] + B.dnt[m, 1] * B.ps[m, 1]
        B.acc[6] += (B.dnt[m, 0] + B.dnt[m, 1]) * float(COLS // 2)


def ph_bwd_two(e, B, steps):
    chunk = 256
    width = 256

    def body(it, _):
        hooks(it, steps)
        at = pl.multiple_of(it * chunk, chunk)
        m = it // (POS // chunk)
        c0 = (it % (POS // chunk)) * (chunk // OWN)
        span = pl.ds(at, chunk)
        lanes = [slice(LANES * j, LANES * (j + 1)) for j in range(J)]
        dz = B.dz[span, :]
        for k in range(HID // width):
            hid = slice(width * k, width * (k + 1))
            du = lax.dot_general(dz, B.wdn[hid, :], (((1,), (1,)), ((), ())), preferred_element_type=F32)
            dh = (du * B.gp[span, hid].astype(F32)).astype(BF16)
            B.gp[span, hid] = dh
            B.acup[:, hid] += fold8(dh.astype(F32))
        dn = lax.dot_general(B.gp[span, :], B.wup[...], (((1,), (1,)), ((), ())), preferred_element_type=F32)
        dns = [dn[:, lanes[j]] for j in range(J)]
        dg = [dns[j] * vec_row(B, 1, j) for j in range(J)]
        hat = [B.v1[span, lanes[j]] for j in range(J)]
        m1 = lane_sum(dg)
        m2 = lane_sum([dg[j] * hat[j] for j in range(J)])
        scale = B.rs1[span, :]
        for j in range(J):
            dy = scale * (dg[j] - m1 - hat[j] * m2)
            B.acc[0, :, lanes[j]] += fold8(dy)
            B.acc[1, :, lanes[j]] += fold8(dns[j] * hat[j])
            B.acc[2, :, lanes[j]] += fold8(dns[j])
            for c in range(chunk // OWN):
                B.big[pl.ds(xrow(j, m) + (3 + c0 + c) * SUB + 3, OWN), :] = dy[OWN * c : OWN * (c + 1), :]
        return 0

    lax.fori_loop(0, NPOS // chunk, body, 0)


def wgrad_down(e, B, f):
    for k in range(2):
        first = 2 * C * f + C * k
        w = lax.dot_general(
            B.u[:, first : first + C], B.dz[...], (((0,), (0,)), ((), ())), preferred_element_type=F32
        )
        w = w.reshape(24, 16, C)
        a, b = w[:, 0:8], w[:, 8:16]
        units = [v[:, :, LANES * j : LANES * (j + 1)] for v in (a, b) for j in range(J)]
        tiles = [jnp.concatenate(units[2 * t : 2 * t + 2], axis=1).astype(BF16) for t in range(3)]
        for q in range(24):
            piece, inner = divmod(24 * k + q, 3)
            for t in range(3):
                B.gb[f, piece // 4, piece // 2 % 2, piece % 2, inner, t] = tiles[t][q]


def wgrad_up(e, B, f):
    width = 256
    for k in range(3):
        first = 768 * (f - 2) + width * k
        w = lax.dot_general(
            B.n[...], B.gp[:, first : first + width], (((0,), (0,)), ((), ())), preferred_element_type=F32
        )
        w = w.reshape(48, 8, width)
        w = jnp.concatenate([w[:, :, :LANES], w[:, :, LANES:]], axis=1).astype(BF16)
        B.gb[f, :, :, :, :, k] = w.reshape(4, 2, 2, 3, 16, LANES)


def dy_copy(e, B, m, up):
    if up:
        return remote(e, B.hs.at[m, 1], B.hr.at[m, 0], B.s_dy.at[1, m], B.r_dy.at[1, m], r=e.r + GROUP)
    return remote(e, B.hs.at[m, 0], B.hr.at[m, 1], B.s_dy.at[0, m], B.r_dy.at[0, m], r=e.r - GROUP)


def dy_send(e, B, m):
    zero = jnp.zeros((3 * SUB, LANES), F32)
    for j in range(J):
        B.big[pl.ds(xrow(j, m), 3 * SUB), :] = zero
        B.big[pl.ds(xrow(j, m) + (COLS + 3) * SUB, 3 * SUB), :] = zero
        for side in range(2):
            for k in range(3):
                row = 3 + k if side == 0 else 8 + k
                v = B.big[pl.ds(xrow(j, m) + 3 * SUB + row, COLS, stride=SUB), :]
                B.hs[m, side, k, :, LANES * j : LANES * (j + 1)] = v.astype(BF16)

    @pl.when(e.g > 0)
    def _():
        dy_copy(e, B, m, False).start()

    @pl.when(e.g < e.G - 1)
    def _():
        dy_copy(e, B, m, True).start()


def ph_dy_edges(e, B):
    zero = jnp.zeros((MICRO, 3, COLS, C), BF16)

    @pl.when(e.g == 0)
    def _():
        B.hr[:, 0] = zero

    @pl.when(e.g == e.G - 1)
    def _():
        B.hr[:, 1] = zero


def dy_take(e, B, m):
    @pl.when(e.g < e.G - 1)
    def _():
        dy_copy(e, B, m, False).wait_recv()

    @pl.when(e.g > 0)
    def _():
        dy_copy(e, B, m, True).wait_recv()

    for j in range(J):
        for side in range(2):
            for k in range(3):
                row = k if side == 0 else 11 + k
                v = B.hr[m, side, k, :, LANES * j : LANES * (j + 1)].astype(F32)
                B.big[pl.ds(xrow(j, m) + 3 * SUB + row, COLS, stride=SUB), :] = v


def ph_dy_done(e, B):
    for m in range(MICRO):

        @pl.when(e.g > 0)
        def _(m=m):
            dy_copy(e, B, m, False).wait_send()

        @pl.when(e.g < e.G - 1)
        def _(m=m):
            dy_copy(e, B, m, True).wait_send()


def ph_conv_kernel(e, B, parts, steps):
    halves = COLS // TILE

    def taps(it, _):
        hooks(it, steps)
        j = it // 7
        a = it % 7

        def body(k, dk):
            m = parts.start + k // halves
            c0 = k % halves * TILE
            dk = list(dk)
            at = j * NPOS + m * POS + c0 * OWN
            xs = [B.xc[pl.ds(pl.multiple_of(at + OWN * c, OWN), OWN), :] for c in range(TILE)]
            for c in range(TILE + 6):
                d = B.big[pl.ds(xrow(j, m) + (c0 + c) * SUB + a, OWN), :]
                for b in range(7):
                    if 0 <= c - b < TILE:
                        dk[b] = dk[b] + d * xs[c - b]
            return tuple(dk)

        zero = jnp.zeros((OWN, LANES), F32)
        dk = lax.fori_loop(0, halves * len(parts), body, (zero,) * 7)
        for b in range(7):
            tap = (6 - a) * 7 + 6 - b
            B.sg[pl.ds(tap * J + j, 1), :] += jnp.sum(dk[b], 0, keepdims=True)
        return 0

    lax.fori_loop(0, 7 * J, taps, 0)


def tap_low(B, t):
    return B.wh[16 * (t // 8) : 16 * (t // 8) + 16, LANES * (t % 8) : LANES * (t % 8 + 1)]


def ph_taps_low(e, B):
    for t in range(49 * J):
        row = B.kb[t]
        B.wh[16 * (t // 8) : 16 * (t // 8) + 16, LANES * (t % 8) : LANES * (t % 8 + 1)] = jnp.concatenate(
            [row, row], axis=0
        ).astype(BF16)


def ph_conv_input(e, B, steps):
    halves = COLS // TILE
    half = TILE // 2

    def body(it, _):
        m = it // halves
        c0 = it % halves * TILE
        for j in range(J):
            hooks(it, {k // J: v for k, v in steps.items() if k % J == j})
            acc = [None] * half
            for a in range(7):
                cols = []
                for c in range(half + 6):
                    at = xrow(j, m) + (c0 + c) * SUB + a
                    pair = [B.big[pl.ds(at, OWN), :], B.big[pl.ds(at + half * SUB, OWN), :]]
                    cols.append(jnp.concatenate(pair, axis=0).astype(BF16))
                for some in (range(0, 4), range(4, 7)):
                    taps = {b: tap_low(B, ((6 - a) * 7 + 6 - b) * J + j) for b in some}
                    for c in range(half):
                        part = [cols[c + b] * taps[b] for b in some]
                        while len(part) > 1:
                            part = [part[k] + part[k + 1] for k in range(0, len(part) - 1, 2)] + part[len(part) // 2 * 2 :]
                        low = part[0].astype(F32)
                        acc[c] = low if acc[c] is None else acc[c] + low
            at = j * NPOS + m * POS + c0 * OWN
            for c in range(half):
                for k in range(2):
                    span = pl.ds(pl.multiple_of(at + OWN * (c + half * k), OWN), OWN)
                    B.dx[span, :] = B.z[span, :] + acc[c][OWN * k : OWN * (k + 1), :]
        return 0

    lax.fori_loop(0, MICRO * halves, body, 0)


def ph_small_fill(e, B):
    for k in range(HID // LANES):
        B.sg[SG_CUP + k : SG_CUP + k + 1, :] = jnp.sum(B.acup[:, LANES * k : LANES * (k + 1)], 0, keepdims=True)
    for v in range(7):
        for j in range(J):
            row = SG_VEC + v * J + j
            B.sg[row : row + 1, :] = jnp.sum(B.acc[v, :, LANES * j : LANES * (j + 1)], 0, keepdims=True)


def out_copy(e, B, m, k, d):
    j = lax.rem(e.i + d, GROUP)
    cols = pl.ds(TILE * k, TILE)
    return remote(
        e,
        B.xg.at[m, pl.ds(3 + 2 * j, 2), cols],
        B.fo.at[m, e.i, :, cols],
        B.s_out.at[m, k, d],
        B.r_out.at[m, k, d],
        r=e.g * GROUP + j,
    )


def own_out_copy(e, B, m, k):
    cols = pl.ds(TILE * k, TILE)
    return pltpu.make_async_copy(
        B.xg.at[m, pl.ds(3 + 2 * e.i, 2), cols], B.fo.at[m, e.i, :, cols], B.s_outown.at[m, k]
    )


def out_send(e, B, m, k):
    for row in range(OWN):
        for j in range(J):
            v = B.dx[pl.ds(j * NPOS + m * POS + k * TILE * OWN + row, TILE, stride=OWN), :]
            B.xg[m, 3 + row, TILE * k : TILE * (k + 1), LANES * j : LANES * (j + 1)] = v.astype(BF16)
    own_out_copy(e, B, m, k).start()
    for d in (2, 3, 1):
        out_copy(e, B, m, k, d).start()


def ph_out_wait(e, B):
    for m in range(MICRO):
        for k in range(COLS // TILE):
            own_out_copy(e, B, m, k).wait()
            for d in range(1, GROUP):
                out_copy(e, B, m, k, d).wait()


PARTS = 4
PIECE = (144, 144, 288, 288)
START = (ROW_DOWN, ROW_DOWN + 16 * 144, ROW_UP, ROW_UP)


def rs_first(e, B, f):
    c = e.i % 2
    return remote(e, B.gb.at[f, :, :, 1 - c], B.ra1.at[f], B.s_rs.at[f, 0], B.r_rs.at[f, 0], r=e.r + 1 - 2 * c)


def rs_second(e, B, f):
    to = e.g * GROUP + lax.rem(e.i + 2, GROUP)
    return remote(e, B.sa2.at[f], B.ra2.at[f], B.s_rs.at[f, 1], B.r_rs.at[f, 1], r=to)


def group_of(e, q):
    return q * (e.G // 4)


def rs_third(e, B, f, q):
    to = group_of(e, q)
    d = lax.rem(to - e.g + e.G, e.G)
    return remote(e, B.sc.at[f, q], B.rc.at[f, d], B.s_rc.at[f, q], B.r_rc.at[f, d], r=to * GROUP + e.i)


def rs_third_wait(e, B, f, d):
    return remote(e, B.sc.at[f, 0], B.rc.at[f, d], B.s_rc.at[f, 0], B.r_rc.at[f, d], r=lax.rem(e.r + GROUP, e.n))


def rs_fourth(e, B, f, d):
    return remote(e, B.rb.at[f, 0], B.rb.at[f, d], B.s_rb.at[f, d], B.r_rb.at[f, d], b=lax.rem(e.b + d, e.nb))


def ends_here(e, body):
    if e.G == 4:
        body()
    else:
        pl.when(e.g % (e.G // 4) == 0)(body)


def rs_step1(e, B, f):
    rs_first(e, B, f).start()


def rs_step2(e, B, f):
    x, c = e.i // 2, e.i % 2
    rs_first(e, B, f).wait_recv()
    for q in range(4):
        B.sa2[f, q] = (B.gb[f, q, 1 - x, c].astype(F32) + B.ra1[f, q, 1 - x].astype(F32)).astype(BF16)
    rs_second(e, B, f).start()
    for q in range(4):
        B.h1[f, q] = B.gb[f, q, x, c].astype(F32) + B.ra1[f, q, x].astype(F32)


def rs_step3(e, B, f):
    rs_second(e, B, f).wait_recv()
    for q in range(4):
        B.h1[f, q] = B.h1[f, q] + B.ra2[f, q].astype(F32)
        B.sc[f, q] = B.h1[f, q].astype(BF16)
    for q in range(4):

        @pl.when(e.g != group_of(e, q))
        def _(q=q):
            rs_third(e, B, f, q).start()


def rs_step4(e, B, f):
    def body():
        total = B.h1[f, e.g // (e.G // 4)]
        for d in range(1, e.G):
            rs_third_wait(e, B, f, d).wait_recv()
            total = total + B.rc[f, d].astype(F32)
        B.rb[f, 0] = total.astype(BF16)
        for d in range(1, e.nb):
            rs_fourth(e, B, f, d).start()

    ends_here(e, body)


def piece_owners(e, f):
    start = START[f] + PIECE[f] * (e.g // (e.G // 4) * 4 + e.i)
    return start // e.slab, (start + PIECE[f] - 1) // e.slab


def own_slot(B, f, slot):
    return B.ro.at[f, slot] if f < 2 else B.ro_up.at[f - 2, slot]


def own_copy(e, B, f, k, owner):
    slot = lax.rem(e.g // (e.G // 4) * 4 + e.i, 16 if f < 2 else 8)
    return remote(e, B.fp.at[f], own_slot(B, f, slot), B.s_ro.at[f, k], B.r_ro.at[f, slot], r=owner)


def own_wait(e, B, f, slot, home):
    remote(e, B.fp.at[f], own_slot(B, f, slot), B.s_ro.at[f, 0], B.r_ro.at[f, slot], r=home).wait_recv()


def rs_step5(e, B, f):
    def body():
        for d in range(1, e.nb):
            rs_fourth(e, B, f, d).wait_recv()
        total = None
        for b in range(e.nb):
            part = B.rb[f, lax.rem(e.b - b + e.nb, e.nb)].astype(F32)
            total = part if total is None else total + part
        B.fp[f] = total.astype(BF16)
        lo, hi = piece_owners(e, f)

        @pl.when(lo != e.r)
        def _():
            own_copy(e, B, f, 0, lo).start()

        @pl.when(jnp.logical_and(hi != lo, hi != e.r))
        def _():
            own_copy(e, B, f, 1, hi).start()

    ends_here(e, body)


def place(B, f, off, tiles):
    for k in range(3):
        for t in range(3):
            for h in range(2):
                unit = 2 * t + h
                tile = tiles[k, t, 8 * h : 8 * h + 8, :].astype(F32)
                if f >= 2:
                    at = pl.ds(MARGIN + off + 96 * k + 6 * (f - 2) + unit, 8, stride=12)
                else:
                    at = pl.ds(MARGIN + off + 48 * k + 24 * (unit // 3) + unit % 3, 8, stride=3)
                B.gf[at, :] = tile


def rs_place(e, B, f):
    for p in range(16):
        off = START[f] + PIECE[f] * p - e.slab * e.r
        home = group_of(e, p // 4) * GROUP + p % 4

        @pl.when(jnp.logical_and(off < e.slab, off + PIECE[f] > 0))
        def _(p=p, off=off, home=home):
            slot = p % (16 if f < 2 else 8)

            @pl.when(e.r != home)
            def _():
                own_wait(e, B, f, slot, home)
                place(B, f, off, B.ro[f, slot] if f < 2 else B.ro_up[f - 2, slot])

            @pl.when(e.r == home)
            def _():
                place(B, f, off, B.fp[f])


def ph_rs_done(e, B):
    for f in range(PARTS):
        rs_first(e, B, f).wait_send()
        rs_second(e, B, f).wait_send()
        for q in range(4):

            @pl.when(e.g != group_of(e, q))
            def _(f=f, q=q):
                rs_third(e, B, f, q).wait_send()

        def body(f=f):
            for d in range(1, e.nb):
                rs_fourth(e, B, f, d).wait_send()
            lo, hi = piece_owners(e, f)

            @pl.when(lo != e.r)
            def _():
                own_copy(e, B, f, 0, lo).wait_send()

            @pl.when(jnp.logical_and(hi != lo, hi != e.r))
            def _():
                own_copy(e, B, f, 1, hi).wait_send()

        ends_here(e, body)


MARGIN = 1792


QUARTER = 80
SEGMENTS = (
    (0, 0, QUARTER, ROW_K),
    (1, 0, 49 * J - QUARTER, ROW_K + QUARTER),
    (2, 0, 7 * J, ROW_VEC),
    (3, 0, HID // LANES, ROW_CUP),
)


def small_group(e, B, d):
    j = lax.rem(e.i + d, GROUP)
    at = pl.ds(pl.multiple_of(j * QUARTER, QUARTER), QUARTER)
    return remote(e, B.sg.at[at], B.sg_group.at[d - 1], B.s_sg.at[d], B.r_sg.at[d], r=e.g * GROUP + j)


def small_line(e, B, d):
    to = lax.rem(e.g + d, e.G)
    return remote(e, B.sg_line.at[0], B.sg_line.at[d], B.s_sgl.at[d], B.r_sgl.at[d], r=to * GROUP + e.i)


def small_batch(e, B, d):
    return remote(e, B.sgb.at[0], B.sgb.at[d], B.s_sgb.at[d], B.r_sgb.at[d], b=lax.rem(e.b + d, e.nb))


def small_back(e, B, q, owner):
    at = pl.ds(q * QUARTER, QUARTER)
    return remote(e, B.sga.at[at], B.sga.at[at], B.s_sgg.at[q], B.r_sgg.at[q], r=owner)


def small_moves(e):
    for q, row, count, flat in SEGMENTS:
        owner = flat // e.slab
        holder = owner // GROUP * GROUP + q
        if owner != holder:
            yield q, holder, owner


def small_step1(e, B):
    for d in (2, 3, 1):
        small_group(e, B, d).start()


def small_step2(e, B):
    total = B.sg[pl.ds(pl.multiple_of(e.i * QUARTER, QUARTER), QUARTER), :]
    for d in range(1, GROUP):
        small_group(e, B, d).wait_recv()
        total = total + B.sg_group[d - 1]
    B.sg_line[0] = total
    for d in range(1, e.G):
        small_line(e, B, d).start()


def small_step3(e, B):
    for d in range(1, e.G):
        small_line(e, B, d).wait_recv()
    total = None
    for level in range(e.G):
        part = B.sg_line[lax.rem(e.g - level + e.G, e.G)]
        total = part if total is None else total + part
    B.sgb[0] = total
    for d in range(1, e.nb):
        small_batch(e, B, d).start()


def small_step4(e, B):
    for d in range(1, e.nb):
        small_batch(e, B, d).wait_recv()
    total = None
    for b in range(e.nb):
        part = B.sgb[lax.rem(e.b - b + e.nb, e.nb)]
        total = part if total is None else total + part
    B.sga[pl.ds(pl.multiple_of(e.i * QUARTER, QUARTER), QUARTER), :] = total
    for q, holder, owner in small_moves(e):

        @pl.when(e.r == holder)
        def _(q=q, owner=owner):
            small_back(e, B, q, owner).start()


def ph_small_place(e, B):
    for q, holder, owner in small_moves(e):

        @pl.when(e.r == owner)
        def _(q=q, holder=holder):
            small_back(e, B, q, holder).wait_recv()

    for q, row, count, flat in SEGMENTS:
        off = MARGIN + flat % e.slab
        at = q * QUARTER + row

        @pl.when(e.r == flat // e.slab)
        def _(off=off, at=at, count=count):
            B.gf[off : off + count, :] = B.sga[at : at + count, :]


def ph_small_done(e, B):
    for d in range(1, GROUP):
        small_group(e, B, d).wait_send()
    for d in range(1, e.G):
        small_line(e, B, d).wait_send()
    for d in range(1, e.nb):
        small_batch(e, B, d).wait_send()
    for q, holder, owner in small_moves(e):

        @pl.when(e.r == holder)
        def _(q=q, owner=owner):
            small_back(e, B, q, owner).wait_send()


def ph_head_grads(e, B):
    parts = GROUP * e.nb
    rows = 16 * parts
    sums = None
    for p in range(parts):
        x = B.pall[p].astype(F32)
        sums = x if sums is None else sums + x
        dd = x[6:9, 0:DOUT]
        B.gp[16 * p : 16 * p + 16, 0:DOUT] = jnp.concatenate([dd, dd, jnp.zeros((10, DOUT), F32)], axis=0).astype(BF16)
        dl = x[9:12, 0:CLSP]
        B.gp[rows + 16 * p : rows + 16 * p + 16, 0:CLSP] = jnp.concatenate(
            [jnp.zeros((6, CLSP), F32), dl, jnp.zeros((7, CLSP), F32)], axis=0
        ).astype(BF16)
    B.pb[...] = sums
    for q in range(4):
        for p in range(parts):
            B.v2[16 * p : 16 * p + 16, :] = B.pall[p, :, C * q : C * (q + 1)].astype(F32)
        for j in range(J):
            t = J * q + j
            B.u[LANES * t : LANES * (t + 1), 0:rows] = B.v2[0:rows, LANES * j : LANES * (j + 1)].T.astype(BF16)
    per = DOUT // LANES
    base = MARGIN - e.slab * e.r

    kc = 288
    low = e.slab * e.r - ROW_DS

    @pl.when(jnp.logical_and(low < 4 * C * per, low + e.slab > 0))
    def _():
        k0 = jnp.clip(low // (16 * per) * 16, 0, 4 * C - kc)
        k0 = pl.multiple_of(k0, 16)
        w = jnp.dot(B.u[pl.ds(k0, kc), 0:rows], B.gp[0:rows, 0:DOUT], preferred_element_type=F32)
        for j in range(per):
            B.gf[pl.ds(base + ROW_DS + per * k0 + j, kc, stride=per), :] = w[:, LANES * j : LANES * (j + 1)]

    low2 = e.slab * e.r - ROW_HEAD

    @pl.when(jnp.logical_and(low2 < DOUT * CLS // LANES, low2 + e.slab > 0))
    def _():
        g0 = jnp.clip(low2 // 125, 0, DOUT // 16 - 16)
        k0 = pl.multiple_of(DOUT + 16 * g0, 16)
        for t in range(8):
            B.big[256 * t : 256 * (t + 1), :] = jnp.dot(
                B.u[pl.ds(k0, 256), 0:rows],
                B.gp[rows : 2 * rows, LANES * t : LANES * (t + 1)],
                preferred_element_type=F32,
            )
        lane = lax.broadcasted_iota(jnp.int32, (16, LANES), 1)
        held = None
        for kk in range(16):
            o = (-CLS * kk) % LANES
            tiles = [B.big[pl.ds(256 * t + kk, 16, stride=16), :] for t in range(8)]
            if o:
                tiles = [pltpu.roll(tile, LANES - o, 1) for tile in tiles]
            for s in range(CLS * kk // LANES, (CLS * kk + CLS - 1) // LANES + 1):
                t0 = (LANES * s - CLS * kk) // LANES
                if o == 0:
                    value = tiles[t0]
                elif t0 < 0:
                    value = tiles[0]
                elif t0 + 1 > 7:
                    value = tiles[t0]
                else:
                    value = jnp.where(lane < LANES - o, tiles[t0], tiles[t0 + 1])
                border = CLS * kk - LANES * s
                if border > 0:
                    value = jnp.where(lane < border, held, value)
                if LANES * (s + 1) > CLS * (kk + 1):
                    held = value
                else:
                    B.gf[pl.ds(base + ROW_HEAD + 125 * g0 + s, 16, stride=125), :] = value

    @pl.when(e.r == ROW_OUT // e.slab)
    def _():
        off = MARGIN + ROW_OUT % e.slab
        for j in range(per):
            at = slice(LANES * j, LANES * (j + 1))
            B.gf[off + j : off + j + 1, :] = B.pb[6:7, at] * e.positions + (
                B.pb[7:8, at] * e.positions + B.pb[8:9, at] * e.positions
            )
            gain = B.pb[12:13, at] + B.pb[13:14, at] + B.pb[14:15, at]
            B.gf[off + per + j : off + per + j + 1, :] = gain
            at = slice(DOUT + LANES * j, DOUT + LANES * (j + 1))
            shift = B.pb[12:13, at] + B.pb[13:14, at] + B.pb[14:15, at]
            B.gf[off + 2 * per + j : off + 2 * per + j + 1, :] = shift

    @pl.when(e.r == ROW_BH // e.slab)
    def _():
        off = MARGIN + ROW_BH % e.slab
        for j in range(CLSP // LANES):
            at = slice(LANES * j, LANES * (j + 1))
            B.gf[off + j : off + j + 1, :] = B.pb[9:10, at] + B.pb[10:11, at] + B.pb[11:12, at]
        rest = FLAT - ROW_BH - CLSP // LANES
        B.gf[off + CLSP // LANES : off + CLSP // LANES + rest, :] = jnp.zeros((rest, LANES), F32)


def norm_copy(e, B, d):
    return remote(e, B.nrm.at[0], B.nrm.at[d], B.s_nrm.at[d], B.r_nrm.at[d], r=lax.rem(e.r + d, e.n))


def squares(v):
    return jnp.sum((v * v).reshape(-1, 8, LANES), 0)


def ph_norm_local(e, B):
    size = 64
    whole = e.slab // size

    def body(k, acc):
        return acc + squares(B.gf[pl.ds(pl.multiple_of(MARGIN + size * k, 8), size), :])

    part = lax.fori_loop(0, whole, body, jnp.zeros((8, LANES), F32))
    v = B.gf[MARGIN + whole * size : MARGIN + e.slab, :]
    B.nrm[0] = part + jnp.broadcast_to(jnp.sum(v * v, 0, keepdims=True) * 0.125, (8, LANES))


def ph_norm(e, B):
    def pieces():
        B.nrm[0] += squares(B.fp[...].astype(F32))

    ends_here(e, pieces)

    @pl.when(e.g == 0)
    def _():
        B.nrm[0] += squares(B.sga[pl.ds(pl.multiple_of(e.i * QUARTER, QUARTER), QUARTER), :])

    for d in range(1, e.n):
        norm_copy(e, B, d).start()


def ph_norm_wait(e, B):
    for d in range(1, e.n):
        norm_copy(e, B, d).wait_recv()
    total = None
    for k in range(e.n):
        part = B.nrm[lax.rem(e.r - k + e.n, e.n)]
        total = part if total is None else total + part
    square = jnp.sum(jnp.sum(total, 0, keepdims=True), 1, keepdims=True)
    B.o_norm[...] = jnp.broadcast_to(jnp.sqrt(square), (8, LANES))
    loss = B.pb[15:16, :]
    loss = loss[:, 0:LANES] + loss[:, LANES : 2 * LANES] + loss[:, 2 * LANES : 3 * LANES]
    B.o_loss[...] = jnp.broadcast_to(loss, (8, LANES))
    for d in range(1, e.n):
        norm_copy(e, B, d).wait_send()


def buffers(e):
    n, G, nb, slab = e.n, e.G, e.nb, e.slab
    tiles = (3, 3, 16, LANES)
    parts = GROUP * nb
    V = pltpu.VMEM
    D = pltpu.SemaphoreType.DMA
    return dict(
        gw=V((n, 2, e.half, LANES), BF16),
        tab=V((TAB_ROWS, LANES), F32),
        big=V((10816, LANES), F32),
        dx=V((8 * DOUT, LANES), F32),
        wup=V((C, HID), BF16),
        wdn=V((HID, C), BF16),
        wds=V((4 * C, DOUT), BF16),
        wh=V((DOUT, CLSP), BF16),
        xg=V((MICRO, 14, COLS, C), BF16),
        xc=V((J * NPOS, LANES), F32),
        kb=V((49 * J, 8, LANES), F32),
        v1=V((NPOS, C), F32),
        rs1=V((NPOS, LANES), F32),
        v2=V((NPOS, C), F32),
        rs2=V((NPOS, LANES), F32),
        n=V((NPOS, C), BF16),
        u=V((NPOS, HID), BF16),
        gp=V((NPOS, HID), BF16),
        z=V((J * NPOS, LANES), F32),
        dz=V((NPOS, C), BF16),
        ps=V((MICRO, 2, OWN, C), F32),
        sl=V((16, C), F32),
        sr=V((G, 16, C), F32),
        dn2=V((32, C), F32),
        dnt=V((MICRO, 2, OWN, C), F32),
        pb=V((16, 4 * C), F32),
        pall=V((parts, 16, 4 * C), BF16),
        acc=V((7, 8, C), F32),
        acup=V((8, HID), F32),
        hs=V((MICRO, 2, 3, COLS, C), BF16),
        hr=V((MICRO, 2, 3, COLS, C), BF16),
        gb=V((PARTS, 4, 2, 2) + tiles, BF16),
        ra1=V((PARTS, 4, 2) + tiles, BF16),
        sa2=V((PARTS, 4) + tiles, BF16),
        ra2=V((PARTS, 4) + tiles, BF16),
        h1=V((PARTS, 4) + tiles, F32),
        sc=V((PARTS, 4) + tiles, BF16),
        rc=V((PARTS, G) + tiles, BF16),
        rb=V((PARTS, nb) + tiles, BF16),
        fp=V((PARTS,) + tiles, BF16),
        ro=V((2, 16) + tiles, BF16),
        ro_up=V((2, 8) + tiles, BF16),
        gf=V((MARGIN + slab + MARGIN, LANES), F32),
        sg=V((SG_ROWS, LANES), F32),
        sg_group=V((GROUP - 1, QUARTER, LANES), F32),
        sg_line=V((G, QUARTER, LANES), F32),
        sgb=V((nb, QUARTER, LANES), F32),
        sga=V((SG_ROWS, LANES), F32),
        nrm=V((n, 8, LANES), F32),
        s_own=D((1,)),
        s_feat=D((MICRO, GROUP)),
        r_feat=D((MICRO, GROUP)),
        s_halo=D((2, MICRO)),
        r_halo=D((2, MICRO)),
        s_tab=D((len(TABLES), G)),
        s_tabg=D((len(TABLES), GROUP)),
        r_tab=D((len(TABLES),)),
        s_line=D((2, G)),
        r_line=D((G, CHUNKS)),
        s_pair=D((G,)),
        r_pair=D((G, CHUNKS)),
        s_row=D((2, G)),
        r_row=D((2, G, CHUNKS)),
        s_core=D((4, G)),
        r_core=D((4, G, CHUNKS)),
        s_patch=D((G,)),
        r_patch=D((G,)),
        s_pb=D((nb,)),
        r_pb=D((nb,)),
        s_pg=D((GROUP,)),
        r_pg=D((GROUP,)),
        s_dy=D((2, MICRO)),
        r_dy=D((2, MICRO)),
        s_out=D((MICRO, 2, GROUP)),
        r_out=D((MICRO, 2, GROUP)),
        s_outown=D((MICRO, 2)),
        s_rs=D((PARTS, 2)),
        r_rs=D((PARTS, 2)),
        s_rc=D((PARTS, 4)),
        r_rc=D((PARTS, G)),
        s_rb=D((PARTS, nb)),
        r_rb=D((PARTS, nb)),
        s_ro=D((PARTS, 2)),
        r_ro=D((PARTS, 16)),
        s_sg=D((GROUP,)),
        r_sg=D((GROUP,)),
        s_sgl=D((G,)),
        r_sgl=D((G,)),
        s_sgg=D((GROUP,)),
        r_sgg=D((GROUP,)),
        s_sgb=D((nb,)),
        r_sgb=D((nb,)),
        s_nrm=D((n,)),
        r_nrm=D((n,)),
    )


def ph_clear(e, B):
    B.sg[...] = jnp.zeros_like(B.sg)
    B.gf[...] = jnp.zeros_like(B.gf)


def ph_result(e, B):
    B.o_grad[...] = B.gf[MARGIN : MARGIN + e.slab, :]


def schedule(e, B):
    def do(step, *args):
        return lambda: step(e, B, *args)

    def level_of(row):
        return row // e.slab // GROUP

    up = range(0, level_of(ROW_CUP - 1) + 1)
    down = range(up.stop, level_of(ROW_VEC - 1) + 1)
    rest = range(down.stop, e.G)
    ph_barrier_signal(e, B)
    ph_cast(e, B)
    ph_feat_zero(e, B)
    ph_clear(e, B)
    ph_barrier_wait(e, B)
    every = range(CHUNKS)
    one, two = range(0, CHUNKS // 2), range(CHUNKS // 2, CHUNKS)

    def hops(some):
        return range(max(max(level, e.G - 1 - level) for level in some) + 1)

    def steps(step, some, which, chunks):
        return [do(step, some, h, chunks) for h in which]

    ph_tables_start(e, B)
    feat_start(e, B, 0)
    line_send(e, B, range(e.G), every)
    tables_forward(e, B, (0, 2))
    feat_start(e, B, 1)
    line_step(e, B, up, 1, every)
    halo_start(e, B, 0)
    feat_start(e, B, 2)
    for h in hops(up)[2:3]:
        line_step(e, B, up, h, every)
    for h in hops(up)[:3]:
        pair_step(e, B, up, h, every)
    tables_wait(e, B, (0, 2))
    ph_taps(e, B)
    ph_conv_fwd(
        e,
        B,
        {
            0: [do(halo_wait, 0), do(transpose, 0)],
            1: [do(halo_start, 1)] + steps(line_step, rest, [1], one),
            2: steps(line_step, rest, [1], two) + steps(line_step, up, hops(up)[3:], every) + steps(pair_step, up, hops(up)[3:], every),
            4: [do(halo_start, 2)] + steps(line_step, down, [1], every) + steps(pair_step, down, hops(down)[:2], every),
            6: [do(halo_wait, 1), do(transpose, 1)],
            7: [do(tables_forward, (1, 3, 4))] + steps(row_step, up, hops(up), one),
            8: steps(line_step, rest, hops(rest)[2:3], one) + steps(pair_step, rest, hops(rest)[:2], every),
            9: steps(row_step, up, hops(up), two),
            10: steps(line_step, rest, hops(rest)[2:3], two),
            11: steps(pair_step, rest, hops(rest)[2:3], every),
            12: [do(halo_wait, 2), do(transpose, 2)]
            + steps(line_step, down, hops(down)[2:], every)
            + steps(pair_step, down, hops(down)[2:], every),
            13: steps(row_step, down, hops(down)[:2], every),
            14: steps(core_step, up, hops(up), one),
            15: steps(line_step, rest, hops(rest)[3:], every) + steps(pair_step, rest, hops(rest)[3:], every),
            16: steps(row_step, rest, [0], every),
            17: steps(core_step, up, hops(up), two),
        },
    )
    ph_norm_one(e, B)
    tables_wait(e, B, (1, 3, 4))
    row_step(e, B, rest, 1, every)
    gather_ready(e, B, up)
    ph_weights_up(e, B)
    ph_mlp_up(
        e,
        B,
        {
            0: steps(row_step, down, hops(down)[2:], every),
            1: steps(row_step, rest, hops(rest)[2:3], every),
            2: steps(core_step, down, hops(down)[:2], every),
            3: steps(row_step, rest, hops(rest)[3:], every) + steps(core_step, rest, [0], every),
            5: steps(core_step, down, hops(down)[2:], every),
        },
    )
    gather_ready(e, B, down)
    ph_weights_down(e, B)
    ph_mlp_down(
        e,
        B,
        {
            0: steps(core_step, rest, [1], every),
            2: steps(core_step, rest, hops(rest)[2:3], every),
            5: steps(core_step, rest, hops(rest)[3:], every),
        },
    )
    ph_patch_local(e, B)
    patch_start(e, B)
    gather_ready(e, B, rest)
    ph_weights_head(e, B)
    patch_wait(e, B)
    ph_head(e, B)
    ph_payload_batch(e, B)
    ph_dy_edges(e, B)
    ph_bwd_one(e, B)
    for f in (0, 1):
        wgrad_down(e, B, f)
        rs_step1(e, B, f)
    ph_bwd_two(
        e,
        B,
        {
            1: [do(ph_payload_group)],
            2: [do(dy_send, 0), do(rs_step2, 0)],
            3: [do(rs_step2, 1)],
            4: [do(dy_send, 1)],
        },
    )
    dy_send(e, B, 2)
    for f in (2, 3):
        wgrad_up(e, B, f)
        rs_step1(e, B, f)
    dy_take(e, B, 0)
    dy_take(e, B, 1)
    rs_step3(e, B, 0)
    ph_conv_kernel(
        e,
        B,
        range(0, MICRO - 1),
        {
            4: [do(rs_step3, 1)],
            6: [do(rs_step2, 2)],
            9: [do(rs_step2, 3)],
            20: [do(rs_step3, 2)],
        },
    )
    dy_take(e, B, MICRO - 1)
    ph_conv_kernel(
        e,
        B,
        range(MICRO - 1, MICRO),
        {
            7: [do(rs_step3, 3)],
            12: [do(rs_step4, 0)],
            17: [do(rs_step4, 1)],
        },
    )
    ph_small_fill(e, B)
    small_step1(e, B)
    ph_feat_done(e, B)
    ph_taps_low(e, B)
    ph_conv_input(
        e,
        B,
        {
            3: [do(out_send, 0, 0)],
            5: [do(rs_step4, 2)],
            6: [do(small_step2), do(out_send, 0, 1)],
            7: [do(rs_step5, 0), do(rs_step4, 3)],
            8: [do(rs_step5, 1)],
            9: [do(rs_step5, 2), do(out_send, 1, 0)],
            11: [do(rs_step5, 3)],
            12: [do(out_send, 1, 1)],
            13: [do(ph_payload_wait), do(ph_head_grads), do(ph_norm_local)],
            14: [do(small_step3)],
            15: [do(out_send, 2, 0)],
        },
    )
    small_step4(e, B)
    ph_norm(e, B)
    out_send(e, B, 2, 1)
    for f in range(PARTS):
        rs_place(e, B, f)
    ph_small_place(e, B)
    ph_result(e, B)
    ph_tables_done(e, B)
    ph_gather_done(e, B)
    ph_dy_done(e, B)
    ph_rs_done(e, B)
    ph_small_done(e, B)
    ph_norm_wait(e, B)
    ph_out_wait(e, B)


def step_kernel(e, names, *refs):
    B = Env()
    for name, ref in zip(names, refs):
        setattr(B, name, ref)
    here(e)
    schedule(e, B)


def train_step(e, features, mask, labels, params):
    bufs = buffers(e)
    names = ["mask", "labels", "features", "params", "o_grad", "o_norm", "o_loss", "fo"] + list(bufs)
    return pl.pallas_call(
        functools.partial(step_kernel, e, names),
        out_shape=(
            jax.ShapeDtypeStruct((e.slab, LANES), F32),
            jax.ShapeDtypeStruct((8, LANES), F32),
            jax.ShapeDtypeStruct((8, LANES), F32),
            jax.ShapeDtypeStruct((MICRO, GROUP, 2, COLS, C), BF16),
        ),
        in_specs=[
            pl.BlockSpec(memory_space=pltpu.SMEM),
            pl.BlockSpec(memory_space=pltpu.SMEM),
            pl.BlockSpec(memory_space=pl.ANY),
            pl.BlockSpec(memory_space=pltpu.VMEM),
        ],
        out_specs=(
            pl.BlockSpec(memory_space=pltpu.VMEM),
            pl.BlockSpec(memory_space=pltpu.VMEM),
            pl.BlockSpec(memory_space=pltpu.VMEM),
            pl.BlockSpec(memory_space=pl.ANY),
        ),
        scratch_shapes=list(bufs.values()),
        compiler_params=pltpu.CompilerParams(collective_id=0, has_side_effects=True, vmem_limit_bytes=64 * MB - 65536),
        name="train_step",
    )(mask, labels, features, params)


def update_kernel(e, norm, loss, grad, params, m1, m2, out, o_norm, o_loss, new_params, first, second, feats, *scratch):
    g, p, a, b, fin, fout, s_in, s_out, s_feat, s_fout = scratch
    parts = 4
    size = e.slab // parts // 8 * 8
    spans = [(k * size, size if k < parts - 1 else e.slab - k * size) for k in range(parts)]
    copy = pltpu.make_async_copy
    ins = []
    for k, (at, count) in enumerate(spans):
        for q, (src, dst) in enumerate(((grad, g), (params, p), (m1, a), (m2, b))):
            ins.append(copy(src.at[pl.ds(at, count)], dst.at[pl.ds(at, count)], s_in.at[k, q]))
            ins[-1].start()
    fins = [copy(out.at[k], fin.at[k], s_feat.at[k]) for k in range(MICRO)]
    for cp in fins:
        cp.start()
    o_norm[0, 0] = jnp.max(norm[...])
    o_loss[0, 0] = jnp.max(loss[...])
    scale = jnp.minimum(1.0, CLIP / (norm[0:1, 0:1] + 1e-06))
    outs = []
    for k, (at, count) in enumerate(spans):
        for q in range(4):
            ins[4 * k + q].wait()
        rows = slice(at, at + count)
        clipped = g[rows, :] * scale
        one = BETA_ONE * a[rows, :] + (1.0 - BETA_ONE) * clipped
        two = BETA_TWO * b[rows, :] + (1.0 - BETA_TWO) * clipped * clipped
        a[rows, :] = one
        b[rows, :] = two
        ratio = one / (1.0 - BETA_ONE**STEP) / (jnp.sqrt(two / (1.0 - BETA_TWO**STEP)) + EPS_ADAM)
        p[rows, :] = p[rows, :] - RATE * (ratio + DECAY * p[rows, :])
        for q, (src, dst) in enumerate(((p, new_params), (a, first), (b, second))):
            outs.append(copy(src.at[pl.ds(at, count)], dst.at[pl.ds(at, count)], s_out.at[k, q]))
            outs[-1].start()
        if k < MICRO:
            fins[k].wait()
            fout[k] = fin[k].astype(F32)
            outs.append(copy(fout.at[k], feats.at[k], s_fout.at[k]))
            outs[-1].start()
    for cp in outs:
        cp.wait()


def update(e, grad, norm, loss, params, m1, m2, out):
    flat = jax.ShapeDtypeStruct((e.slab, LANES), F32)
    scalar = jax.ShapeDtypeStruct((1, 1), F32)
    shape = (MICRO, GROUP, 2, COLS, C)
    near, far, one = (pl.BlockSpec(memory_space=k) for k in (pltpu.VMEM, pl.ANY, pltpu.SMEM))
    D = pltpu.SemaphoreType.DMA
    return pl.pallas_call(
        functools.partial(update_kernel, e),
        in_specs=[near, near, far, far, far, far, far],
        out_specs=(one, one, far, far, far, far),
        out_shape=(scalar, scalar, flat, flat, flat, jax.ShapeDtypeStruct(shape, F32)),
        scratch_shapes=[pltpu.VMEM((e.slab, LANES), F32)] * 4
        + [pltpu.VMEM(shape, BF16), pltpu.VMEM(shape, F32), D((4, 4)), D((4, 3)), D((MICRO,)), D((MICRO,))],
        compiler_params=pltpu.CompilerParams(vmem_limit_bytes=64 * MB - 65536),
        name="update",
    )(norm, loss, grad, params, m1, m2, out)


def local(e, features, drop_mask, labels, params, moment1, moment2):
    flat = [v.reshape(e.slab, LANES) for v in (params, moment1, moment2)]
    grad, norm, loss, out = train_step(e, features, drop_mask, labels, flat[0])
    norm, loss, new_params, first, second, feats = update(e, grad, norm, loss, *flat, out)
    size = e.slab * LANES
    return (
        new_params.reshape(size),
        first.reshape(size),
        second.reshape(size),
        loss.reshape(()),
        norm.reshape(()),
        feats,
    )


def solution(mesh):
    e = Env()
    e.n = mesh.shape["rows"]
    e.nb = mesh.shape["batch"]
    e.G = e.n // GROUP
    e.slab = FLAT // e.n
    e.half = (e.slab + 31) // 32 * 16
    e.positions = float(e.n * COLS // 2)
    e.inv_count = 1.0 / (MICRO * GROUP * e.nb)
    return jax.shard_map(
        functools.partial(local, e),
        mesh=mesh,
        in_specs=(
            P(None, "batch", "rows", None, None),
            P(None, "batch"),
            P(None, "batch"),
            P("rows"),
            P("rows"),
            P("rows"),
        ),
        out_specs=(P("rows"), P("rows"), P("rows"), P(), P(), P(None, "batch", "rows", None, None)),
        check_vma=False,
    )
```

profile of v0, /device:TPU:0, one launch (start us, length us, event | category | flops | bytes accessed | tf_op | source)
XLA Modules:
  0.0 125.9 jit_solution(10244512347033930412)
XLA Ops:
  0.6 119.6 %train_step.1 = (f32[1540,128]{1,0:T(8,128)}, f32[8,128]{1,0:T(8,128)}, f32[8,128]{1,0:T(8,128)}, bf16[3,4,2,64,384]{4,3,2,1,0:T(8,128)(2,1)}) custom-call(s32[3,4]{1,0:T(4,128)} %refs_0_.1, s32[3,4]{1,0:T(4,128)} %refs_1_.1, bf16[3,4,2,64,384]{4,3,2,1,0:T(8,128)(2,1)} %refs_2_.1, f32[1540,128]{1,0:T(8,128)} %bitcast.8), custom_call_target="tpu_custom_call" | custom-call | tf_op jit(solution)/shard_map/train_step/pallas_call | solution.py:1814
  120.2 5.5 %update.1 = (f32[1,1]{1,0:T(1,128)}, f32[1,1]{1,0:T(1,128)}, f32[1540,128]{1,0:T(8,128)}, f32[1540,128]{1,0:T(8,128)}, f32[1540,128]{1,0:T(8,128)}, /*index=5*/f32[3,4,2,64,384]{4,3,2,1,0:T(8,128)}) custom-call(f32[8,128]{1,0:T(8,128)} %get-tuple-element.16.norm, f32[8,128]{1,0:T(8,128)} %get-tuple-element.17.loss, f32[1540,128]{1,0:T(8,128)} %get-tuple-element.18.grad, ...), custom_call_target="tpu_custom_call" | custom-call | tf_op jit(solution)/shard_map/update/pallas_call | solution.py:1887
where the time goes:
time: 126 us
  Pallas kernels  125 us (99%)
    pallas_call x1, Pallas kernels, train_step(): pl.pallas_call(functools.partial(step_kernel, e, names), out_shape=(jax.S...  120 us
    pallas_call x1, Pallas kernels, update(): pl.pallas_call(functools.partial(update_kernel, e), in_specs=[near, near,...  5.46 us

commit v1 on v0

--- a/solution.py
+++ b/solution.py
@@ -282,7 +282,7 @@
                 table_group(e, B, k, d).wait_send()
 
 
-CHUNKS = 4
+CHUNKS = 2
 
 
 def chunk_of(e, c):
@@ -1779,11 +1779,13 @@
             9: [do(rs_step5, 2), do(out_send, 1, 0)],
             11: [do(rs_step5, 3)],
             12: [do(out_send, 1, 1)],
-            13: [do(ph_payload_wait), do(ph_head_grads), do(ph_norm_local)],
-            14: [do(small_step3)],
+            13: [do(small_step3)],
             15: [do(out_send, 2, 0)],
         },
     )
+    ph_payload_wait(e, B)
+    ph_head_grads(e, B)
+    ph_norm_local(e, B)
     small_step4(e, B)
     ph_norm(e, B)
     out_send(e, B, 2, 1)

time: 126 us -> 126 us (level)
  no operation moved by 1% of the time
where the time goes in v1:
time: 126 us
  Pallas kernels  125 us (99%)
    pallas_call x1, Pallas kernels, train_step(): pl.pallas_call(functools.partial(step_kernel, e, names), out_shape=(jax.S...  119 us
    pallas_call x1, Pallas kernels, update(): pl.pallas_call(functools.partial(update_kernel, e), in_specs=[near, near,...  5.46 us

profile of v1, /device:TPU:0, one launch (start us, length us, event | category | flops | bytes accessed | tf_op | source)
XLA Modules:
  0.0 125.7 jit_solution(2916710254940976452)
XLA Ops:
  0.6 119.4 %train_step.1 = (f32[1540,128]{1,0:T(8,128)}, f32[8,128]{1,0:T(8,128)}, f32[8,128]{1,0:T(8,128)}, bf16[3,4,2,64,384]{4,3,2,1,0:T(8,128)(2,1)}) custom-call(s32[3,4]{1,0:T(4,128)} %refs_0_.1, s32[3,4]{1,0:T(4,128)} %refs_1_.1, bf16[3,4,2,64,384]{4,3,2,1,0:T(8,128)(2,1)} %refs_2_.1, f32[1540,128]{1,0:T(8,128)} %bitcast.8), custom_call_target="tpu_custom_call" | custom-call | tf_op jit(solution)/shard_map/train_step/pallas_call | solution.py:1816
  120.1 5.5 %update.1 = (f32[1,1]{1,0:T(1,128)}, f32[1,1]{1,0:T(1,128)}, f32[1540,128]{1,0:T(8,128)}, f32[1540,128]{1,0:T(8,128)}, f32[1540,128]{1,0:T(8,128)}, /*index=5*/f32[3,4,2,64,384]{4,3,2,1,0:T(8,128)}) custom-call(f32[8,128]{1,0:T(8,128)} %get-tuple-element.16.norm, f32[8,128]{1,0:T(8,128)} %get-tuple-element.17.loss, f32[1540,128]{1,0:T(8,128)} %get-tuple-element.18.grad, ...), custom_call_target="tpu_custom_call" | custom-call | tf_op jit(solution)/shard_map/update/pallas_call | solution.py:1889
